TPU v7x, 1024 devices: a whole 8x8x8 slice. The times are simulated.
1024 devices in a mesh: expert: 64 (over x, y_lo, core), tensor: 16 (over z, y_hi).
Axes of the slice: x: 8, y: 8 (y_hi: 2, y_lo: 4; y = y_hi * 4 + y_lo), z: 8, core: 2. Of those that a mesh axis runs over, the one named last changes fastest.
Arguments:
- out_grad: bfloat16 [16384, 3584], P('expert', 'tensor'), may hold values from -6 to 6
- router_logits: float32 [16384, 2], P('expert'), may hold values from -6 to 6
- expert_ids: int32 [16384, 2], P('expert'), may hold values from 0 to 63, as said below
- slot_ids: int32 [16384, 2], P('expert'), may hold values from 0 to 11, as said below
- down_weight: bfloat16 [64, 2432, 3584], P('expert', 'tensor'), may hold values from -0.125 to 0.125
- gate_pre: bfloat16 [64, 768, 2432], P('expert', None, 'tensor'), may hold values from -6 to 6
- up_pre: bfloat16 [64, 768, 2432], P('expert', None, 'tensor'), may hold values from -6 to 6
Outputs:
- down_grad: bfloat16 [64, 2432, 3584], P('expert', 'tensor')
- gate_grad: bfloat16 [64, 768, 2432], P('expert', None, 'tensor')
- up_grad: bfloat16 [64, 768, 2432], P('expert', None, 'tensor')
- router_grad: float32 [16384, 2], P('expert')
Inputs may be any that keep to these rules, and one draw needn't show every extreme that they name: `expert_ids`: the two experts of a token differ. Within each block of 256 consecutive tokens no expert is named by more than 12 tokens, and one expert, the same in all blocks, is named by exactly 12 tokens in every block. `slot_ids`: within each block of 256 consecutive tokens, the n tokens that name an expert carry the slots 0 to n - 1 for it, each once.
All inputs are finite; a program needn't handle non-finite values.
Results may differ from a plain program's by a relative error of at most 0.0056.
Values may be sent and summed in bfloat16 or wider, within the bound.
A program may use at most 32 MiB of HBM per device.

v0:
```python
import jax
import jax.numpy as jnp
from jax import lax
from jax.sharding import PartitionSpec as P


def lookup(matches, probe_table):
    return jnp.sum(jnp.where(matches, probe_table[None, None, :], 0.0), axis=2)


def shards(out_grad, router_logits, expert_ids, slot_ids, down_weight, gate_pre, up_pre):
    gate_share = jax.nn.sigmoid(router_logits[:, 0] - router_logits[:, 1])
    combine = jnp.stack([gate_share, 1.0 - gate_share], 1).astype(jnp.bfloat16)
    expert_count = lax.axis_size("expert")
    slot_rows = gate_pre.shape[1]
    capacity = slot_rows // expert_count
    slot_index = expert_ids * capacity + slot_ids
    positions = lax.broadcasted_iota(jnp.int32, (1, 1, slot_rows), 2)
    matches = slot_index[:, :, None] == positions
    selector = matches.astype(jnp.bfloat16)
    outgoing = jnp.einsum(
        "tkr,td->rd", selector, out_grad, preferred_element_type=jnp.float32
    ).astype(jnp.bfloat16)
    outgoing_weight = jnp.einsum(
        "tkr,tk->r", selector, combine, preferred_element_type=jnp.float32
    ).astype(jnp.bfloat16)
    grad_rows, arrived_weight = (
        lax.all_to_all(
            outgoing.reshape(expert_count, capacity, outgoing.shape[1]),
            "expert",
            split_axis=0,
            concat_axis=0,
            tiled=True,
        ),
        lax.all_to_all(
            outgoing_weight.reshape(expert_count, capacity),
            "expert",
            split_axis=0,
            concat_axis=0,
            tiled=True,
        ),
    )
    grad_rows = grad_rows.reshape(slot_rows, outgoing.shape[1])
    slot_weight = arrived_weight.reshape(slot_rows, 1).astype(jnp.float32)
    weight = down_weight[0]
    gate_f = gate_pre[0].astype(jnp.float32)
    up_f = up_pre[0].astype(jnp.float32)
    sigma_gate = jax.nn.sigmoid(gate_f)
    silu_gate = gate_f * sigma_gate
    activation = silu_gate * up_f
    scaled = (slot_weight * activation).astype(jnp.bfloat16)
    full_rows = lax.all_gather(grad_rows, "tensor", axis=1, tiled=True)
    hidden_back = lax.dot_general(
        full_rows, weight, (((1,), (1,)), ((), ())), preferred_element_type=jnp.float32
    )
    down_acc = lax.dot_general(
        scaled, full_rows, (((0,), (0,)), ((), ())), preferred_element_type=jnp.float32
    )
    row_probe = jnp.sum(hidden_back * activation, axis=1)
    hidden_grad = slot_weight * hidden_back
    gate_grad = (hidden_grad * up_f * (sigma_gate * (1.0 + gate_f * (1.0 - sigma_gate)))).astype(
        jnp.bfloat16
    )
    up_grad = (hidden_grad * silu_gate).astype(jnp.bfloat16)
    down_grad = down_acc.astype(jnp.bfloat16)
    total_probe = lax.psum(row_probe, "tensor")
    probe_table = lax.all_to_all(
        total_probe.reshape(expert_count, capacity),
        "expert",
        split_axis=0,
        concat_axis=0,
        tiled=True,
    )
    token_probe = lookup(matches, probe_table.reshape(slot_rows))
    slope = (token_probe[:, 0] - token_probe[:, 1]) * gate_share * (1.0 - gate_share)
    router_grad = jnp.stack([slope, -slope], 1)
    return (down_grad[None], gate_grad[None], up_grad[None], router_grad)


def solution(mesh):
    placed = (
        P("expert", "tensor"),
        P("expert", None),
        P("expert", None),
        P("expert", None),
        P("expert", "tensor", None),
        P("expert", None, "tensor"),
        P("expert", None, "tensor"),
    )
    return jax.shard_map(
        shards,
        mesh=mesh,
        in_specs=placed,
        out_specs=(
            P("expert", "tensor", None),
            P("expert", None, "tensor"),
            P("expert", None, "tensor"),
            P("expert", None),
        ),
        check_vma=False,
    )
```

profile of v0, /device:TPU:1, one launch (start us, length us, event | category | flops | bytes accessed | tf_op | source)
XLA Modules:
  0.0 351.9 jit_solution(15351597715947660053)
XLA Ops:
  7.2 0.0 copy-start
  7.2 0.0 all-gather.2.cloned.1.call-start
  7.2 0.8 multiply_add_fusion
  8.0 0.2 convert_reduce_fusion
  8.2 1.2 fusion.24
  9.4 0.2 copy.20
  9.6 0.1 reshape.40
  9.7 0.0 copy-start.1
  9.7 0.0 copy-start.2
  9.7 35.4 %all_to_all.24 = bf16[64,12,224]{2,1,0:T(8,128)(2,1)S(1)} all-to-all(bf16[64,12,224]{2,1,0:T(8,128)(2,1)S(1)} %reshape.40), channel_id=1, replica_groups=mesh['expert'=64,'tensor'=16] {'expert'}, dimensions={0} | all-to-all | bytes 688128 | tf_op jit(solution)/shard_map/all_to_all | solution.py:28
  45.1 0.2 reshape.41
  45.3 0.9 copy.21
  46.2 0.0 all-gather.2.cloned.1.call-update
  46.2 0.0 copy-start.3
  46.2 152.0 %all-gather.2.cloned.1.call-done = bf16[768,3584]{0,1:T(8,128)(2,1)} async-done(((bf16[768,224]{0,1:T(8,128)(2,1)}), bf16[768,3584]{0,1:T(8,128)(2,1)}) %all-gather.2.cloned.1.call-update) | async-done | bytes 5505040 | tf_op jit(solution)/shard_map/all_gather | solution.py:52
  198.2 3.6 %multiply_reduce_fusion = (f32[768]{0:T(1024)S(1)}, f32[768,152]{0,1:T(8,128)S(1)}) fusion(bf16[1,768,152]{1,2,0:T(8,128)(2,1)S(1)} %copy-done.1, bf16[1,768,152]{1,2,0:T(8,128)(2,1)S(1)} %copy-done.2, bf16[768,3584]{0,1:T(8,128)(2,1)} %all-gather.2.cloned.1.call-done, bf16[1,152,3584]{2,1,0:T(8,128)(2,1)S(1)} %copy-done), kind=kOutput, calls=%fused_computation.24 | convolution fusion | flops 837813504 | bytes 7531520 | tf_op jit(solution)/shard_map/dot_general | solution.py:53
  201.9 0.1 all_to_all.18
  202.0 77.9 %psum.7 = f32[64,1,12]{2,0,1:T(8,128)S(1)} all-reduce(f32[64,1,12]{2,0,1:T(8,128)S(1)} %all_to_all.18), channel_id=1, replica_groups=mesh['expert'=64,'tensor'=16] {'tensor'}, use_global_device_ids=true, to_apply=%region_2.0 | all-reduce | flops 768 | bytes 6144 | tf_op jit(solution)/shard_map/psum | solution.py:66
  279.9 41.2 %all_to_all.25 = f32[64,1,12]{2,1,0:T(1,128)S(1)} all-to-all(f32[64,1,12]{2,1,0:T(1,128)S(1)} %bitcast.41), channel_id=1, replica_groups=mesh['expert'=64,'tensor'=16] {'expert'}, dimensions={0} | all-to-all | bytes 6144 | tf_op jit(solution)/shard_map/all_to_all | solution.py:67
  321.1 0.5 broadcast.41
  321.6 0.7 reduce.9
  322.3 0.1 broadcast_in_dim.27
  322.4 0.3 select_reduce_fusion
  322.8 0.4 fusion.3
  323.2 0.7 all_to_all.20
  324.0 4.7 %all-to-all-start = ((bf16[64,1,12]{2,1,0:T(2,128)(2,1)}), bf16[64,1,12]{2,1,0:T(2,128)(2,1)S(1)}, u32[]{:S(2)}, u32[]{:S(2)}) async-start(bf16[64,1,12]{2,1,0:T(2,128)(2,1)} %all_to_all.20), calls=%async_computation | async-start | bytes 65536 | tf_op jit(solution)/shard_map/all_to_all | solution.py:35
  328.7 0.6 pad_maximum_fusion
  329.3 9.1 %all-to-all-done = bf16[64,1,12]{2,1,0:T(2,128)(2,1)S(1)} async-done(((bf16[64,1,12]{2,1,0:T(2,128)(2,1)}), bf16[64,1,12]{2,1,0:T(2,128)(2,1)S(1)}, u32[]{:S(2)}, u32[]{:S(2)}) %all-to-all-start) | async-done | bytes 1568 | tf_op jit(solution)/shard_map/all_to_all | solution.py:35
  338.3 0.1 convert_reduce_fusion.1
  338.4 0.1 reshape.42
  338.5 1.0 fusion.14
  339.6 5.5 %fusion = bf16[1,152,3584]{2,1,0:T(8,128)(2,1)} fusion(bf16[768,3584]{0,1:T(8,128)(2,1)} %all-gather.2.cloned.1.call-done, bf16[1,768,152]{1,2,0:T(8,128)(2,1)S(1)} %copy-done.1, f32[768]{0:T(1024)S(1)} %reshape.42, bf16[1,768,152]{1,2,0:T(8,128)(2,1)S(1)} %copy-done.2), kind=kOutput, calls=%fused_computation.1 | convolution fusion | flops 838359040 | bytes 7064576 | tf_op jit(solution)/shard_map/dot_general | solution.py:56
  (7 shorter events, 0.0 us)
Async XLA Ops:
  7.2 191.1 %copy-start = (bf16[1,152,3584]{2,1,0:T(8,128)(2,1)S(1)}, bf16[1,152,3584]{2,1,0:T(8,128)(2,1)}, u32[]{:S(2)}) copy-start(bf16[1,152,3584]{2,1,0:T(8,128)(2,1)} %param.11) | copy-start | bytes 3268612
  7.2 191.1 %all-gather.2.cloned.1.call-start = ((), (), s32[]{:S(2)}) async-start(), calls=%async_computation.3 | async-start | bytes 5849088 | tf_op jit(solution)/shard_map/all_gather | solution.py:52
  9.7 188.5 %copy-start.1 = (bf16[1,768,152]{1,2,0:T(8,128)(2,1)S(1)}, bf16[1,768,152]{1,2,0:T(8,128)(2,1)}, u32[]{:S(2)}) copy-start(bf16[1,768,152]{1,2,0:T(8,128)(2,1)} %param.13) | copy-start | bytes 700420
  9.7 188.5 %copy-start.2 = (bf16[1,768,152]{1,2,0:T(8,128)(2,1)S(1)}, bf16[1,768,152]{1,2,0:T(8,128)(2,1)}, u32[]{:S(2)}) copy-start(bf16[1,768,152]{1,2,0:T(8,128)(2,1)} %param.12) | copy-start | bytes 700420
  46.2 276.5 %copy-start.3 = (f32[256,2]{0,1:T(2,128)S(1)}, f32[256,2]{0,1:T(2,128)}, u32[]{:S(2)}) copy-start(f32[256,2]{0,1:T(2,128)} %param.8) | copy-start | bytes 6148
  324.0 14.4 %all-to-all-start = ((bf16[64,1,12]{2,1,0:T(2,128)(2,1)}), bf16[64,1,12]{2,1,0:T(2,128)(2,1)S(1)}, u32[]{:S(2)}, u32[]{:S(2)}) async-start(bf16[64,1,12]{2,1,0:T(2,128)(2,1)} %all_to_all.20), calls=%async_computation | async-start | bytes 65536 | tf_op jit(solution)/shard_map/all_to_all | solution.py:35
Sparse Core Ops, SparseCore 0:
  46.3 151.8 all-gather.1
where the time goes:
time: 352 us
  waiting for transfers between devices  161 us (46%)
  blocking collectives  154 us (44%)
  between operations  14.2 us (4%)
  matrix products  10.7 us (3%)
  starting transfers between devices  4.73 us (1%)
  other arithmetic  3.78 us (1%)
    all_gather x1, waiting for transfers between devices, shards(): full_rows = lax.all_gather(grad_rows, 'tensor', axis=1, tiled=True)  152 us
    psum x1, blocking collectives, shards(): total_probe = lax.psum(row_probe, 'tensor')  77.9 us
    all_to_all x1, blocking collectives, shards(): lax.all_to_all(total_probe.reshape(expert_count, capacity), 'expert', spl...  41.2 us
    all_to_all x1, blocking collectives, shards(): lax.all_to_all(outgoing.reshape(expert_count, capacity, outgoing.shape[1]...  35.4 us
    all_to_all x1, waiting for transfers between devices, shards(): lax.all_to_all(outgoing_weight.reshape(expert_count, capacity), 'expert',...  9.08 us
  transfers between devices with their start and end apart: 2, of which 2 were waited for; matrix products, arithmetic and copies ran while one was open for 0% of the time, Pallas kernels for 0%

commit v1 on v0

v1 whole, which is shorter than its diff:
```python
import functools

import jax
import jax.numpy as jnp
from jax import lax
from jax.experimental import pallas as pl
from jax.experimental.pallas import tpu as pltpu
from jax.sharding import PartitionSpec as P

MESH = pl.DeviceIdType.MESH
BF16 = jnp.bfloat16
F32 = jnp.float32
LANES = 128


def dot(a, b, contract=((1,), (0,)), precision=None):
    return lax.dot_general(
        a, b, (contract, ((), ())), preferred_element_type=F32, precision=precision
    )


def iota(shape, dim):
    return lax.broadcasted_iota(jnp.int32, shape, dim)


def kernel(
    dims, og, rl, ei, si, w_hbm, gp_hbm, up_hbm, dg_hbm, gg_hbm, ug_hbm, rg,
    w, gp, up, dg, gg, ug,
    perm, ext, xs, xr, ys, yr, g, wp, dgp, hid, act, f1, f2, scaled_t,
    vz, vy, vx, vsum, usum, load_sem, store_sem,
    xsend, xrecv, ysend, yrecv, zsend, zrecv, pzsend, pzrecv, pysend, pyrecv, pxsend, pxrecv,
):
    nx, ny, nc, nz, cap = dims
    nb = ny * nc
    group = nb * cap
    rows = nx * group
    feats = og.shape[1]
    head = feats - LANES
    hidden = w.shape[0]
    e, t = lax.axis_index("expert"), lax.axis_index("tensor")
    x, b = e // nb, e % nb
    z, half = t // 2, t % 2

    def xpeer(i):
        return lax.rem(x + i, nx)

    def bpeer(i):
        return lax.rem(b + i, nb)

    def zpeer(i):
        return lax.rem(z + i + nz, nz)

    def device(x_, b_, z_, half_):
        return {"expert": x_ * nb + b_, "tensor": z_ * 2 + half_}

    def remote(src, dst, send, recv, where):
        return pltpu.make_async_remote_copy(
            src_ref=src, dst_ref=dst, send_sem=send, recv_sem=recv,
            device_id=where, device_id_type=MESH,
        )

    loads = [
        pltpu.make_async_copy(gp_hbm.at[0], gp, load_sem.at[0]),
        pltpu.make_async_copy(up_hbm.at[0], up, load_sem.at[1]),
        pltpu.make_async_copy(w_hbm.at[0], w, load_sem.at[2]),
    ]
    for copy in loads:
        copy.start()

    barrier = pltpu.get_barrier_semaphore()
    peers = [device(xpeer(i), b, z, half) for i in range(1, nx)]
    peers += [device(x, bpeer(i), z, half) for i in range(1, nb)]
    peers += [device(x, bpeer(i), z, 1 - half) for i in range(nb)]
    peers += [device(x, b, zpeer(i), half) for i in range(1, nz)]
    for peer in peers:
        pl.semaphore_signal(barrier, inc=1, device_id=peer, device_id_type=MESH)

    share = jax.nn.sigmoid(rl[:, 0:1] - rl[:, 1:2])
    combine = [share.astype(BF16), (1.0 - share).astype(BF16)]
    tokens = og.shape[0]
    outgoing = None
    for k in range(2):
        ext[k, :, 0:head] = og[:, 0:head]
        ext[k, :, LANES : 2 * LANES] = og[:, head:feats]
        ext[k, :, head:LANES] = jnp.where(
            iota((tokens, LANES - head), 1) == 0, combine[k].astype(F32), 0.0
        ).astype(BF16)
        slot = ei[:, k : k + 1] * cap + si[:, k : k + 1]
        chosen = (iota((tokens, rows), 1) == slot).astype(F32).astype(BF16)
        part = dot(chosen, ext[k], ((0,), (0,)))
        outgoing = part if outgoing is None else outgoing + part
    outgoing = outgoing.astype(BF16)
    for c in range(2):
        xs[c] = outgoing[:, c * LANES : (c + 1) * LANES].reshape(nx, group, LANES)

    pl.semaphore_wait(barrier, len(peers))

    xcopies = [
        [
            remote(xs.at[c, xpeer(i)], xr.at[c, x], xsend.at[c, i], xrecv.at[c, x],
                   device(xpeer(i), b, z, half))
            for i in range(1, nx)
        ]
        for c in range(2)
    ]
    for c in range(2):
        for copy in xcopies[c]:
            copy.start()

    i_row = iota((rows, 1), 0)
    major = i_row // (nx * cap)
    rest = i_row - major * (nx * cap)
    minor = rest // cap
    source = minor * group + major * cap + (rest - minor * cap)
    perm[...] = (iota((rows, rows), 1) == source).astype(F32).astype(BF16)

    ycopies = [[None, None], [None, None]]
    for c in range(2):
        xr[c, x] = xs[c, x]
        for i in range(1, nx):
            remote(xs.at[c, x], xr.at[c, xpeer(i)], xsend.at[c, i], xrecv.at[c, xpeer(i)],
                   device(xpeer(i), b, z, half)).wait_recv()
        turned = dot(perm[...], xr[c].reshape(rows, LANES)).astype(BF16)
        ys[c] = turned.reshape(nb, nx * cap, LANES)
        yr[0, c, b] = ys[c, b]
        ycopies[0][c] = [
            remote(ys.at[c, bpeer(i)], yr.at[0, c, b], ysend.at[0, c, i], yrecv.at[0, c, b],
                   device(x, bpeer(i), z, half))
            for i in range(1, nb)
        ]
        for copy in ycopies[0][c]:
            copy.start()
    for c in range(2):
        ycopies[1][c] = [
            remote(ys.at[c, bpeer(i)], yr.at[1, c, b], ysend.at[1, c, i], yrecv.at[1, c, b],
                   device(x, bpeer(i), z, 1 - half))
            for i in range(nb)
        ]
        for copy in ycopies[1][c]:
            copy.start()

    for copy in loads:
        copy.wait()
    for s in range(2 * nz):
        wp[s, :, 0:head] = w[:, s * feats : s * feats + head]
        wp[s, :, head:LANES] = jnp.zeros((hidden, LANES - head), BF16)
        wp[s, :, LANES : 2 * LANES] = w[:, s * feats + head : (s + 1) * feats]

    longer, shorter = nz // 2, nz - 1 - nz // 2
    hops = [(longer, shorter), (shorter, longer), (shorter, longer), (longer, shorter)]
    zcopies = []

    def zsend_start(q, src, way):
        to = zpeer(1) if way == 0 else zpeer(-1)
        copy = remote(g.at[src, q], g.at[src, q], zsend.at[way, q, src], zrecv.at[q, src],
                      device(x, b, to, half))
        copy.start()
        zcopies.append(copy)

    def zwait(q, src):
        remote(g.at[src, q], g.at[src, q], zsend.at[0, q, src], zrecv.at[q, src],
               device(x, b, zpeer(1), half)).wait_recv()

    hid[...] = jnp.zeros_like(hid)

    def work(q, src):
        h, c = q // 2, q % 2
        shard = src * 2 + (half if h == 0 else 1 - half)
        block = g[src, q]
        cols = slice(c * LANES, (c + 1) * LANES)
        hid[...] += dot(block, wp[shard, :, cols], ((1,), (1,)))
        dgp[shard, :, cols] = dot(scaled_t[...], block).astype(BF16)

    for d in range(4 + nz // 2):
        ready = []
        if d < 4:
            h, c = d // 2, d % 2
            for i in range(1 if h == 0 else 0, nb):
                remote(ys.at[c, b], yr.at[h, c, bpeer(i)], ysend.at[h, c, i],
                       yrecv.at[h, c, bpeer(i)], device(x, bpeer(i), z, half)).wait_recv()
            canon = dot(perm[...], yr[h, c].reshape(rows, LANES),
                        ((0,), (0,)) if nx != nb else ((1,), (0,)))
            g[z, d] = canon.astype(BF16)
            zsend_start(d, z, 0)
            zsend_start(d, z, 1)
            ready.append((d, z))
        for q in range(4):
            s = d - q
            if s < 1:
                continue
            for way in range(2):
                if s <= hops[q][way]:
                    src = zpeer(-s) if way == 0 else zpeer(s)
                    zwait(q, src)
                    if s < hops[q][way]:
                        zsend_start(q, src, way)
                    ready.append((q, src))
        if d == 0:
            slot_weight = g[z, 0, :, head : head + 1].astype(F32)
            gate = gp[...].astype(F32)
            upf = up[...].astype(F32)
            sigma = jax.nn.sigmoid(gate)
            silu = gate * sigma
            act[...] = silu * upf
            scaled = (slot_weight * act[...]).astype(BF16)
            scaled_t[...] = jnp.transpose(scaled)
            f1[...] = slot_weight * (upf * (sigma * (1.0 + gate * (1.0 - sigma))))
            f2[...] = slot_weight * silu
        for q, src in ready:
            work(q, src)

    probe = jnp.sum(hid[...] * act[...], axis=1, keepdims=True)
    i_row = iota((rows, 1), 0)
    i_x = i_row // group
    i_rest = i_row - i_x * group
    i_b = i_rest // cap
    i_lane = i_x * cap + (i_rest - i_b * cap)
    spread = jnp.where(iota((rows, LANES), 1) == i_lane, probe, 0.0)
    j_row = iota((1, rows), 1)
    j_rest = j_row - (j_row // group) * group
    gather = (iota((nb, rows), 0) == j_rest // cap).astype(F32)
    vz[z] = dot(gather, spread, precision=lax.Precision.HIGHEST)
    pz = [
        remote(vz.at[z], vz.at[z], pzsend.at[i], pzrecv.at[z], device(x, b, zpeer(i), half))
        for i in range(1, nz)
    ]
    for copy in pz:
        copy.start()

    gg[...] = (hid[...] * f1[...]).astype(BF16)
    ug[...] = (hid[...] * f2[...]).astype(BF16)
    stores = [
        pltpu.make_async_copy(gg, gg_hbm.at[0], store_sem.at[0]),
        pltpu.make_async_copy(ug, ug_hbm.at[0], store_sem.at[1]),
    ]
    for copy in stores:
        copy.start()

    for i in range(1, nz):
        remote(vz.at[z], vz.at[zpeer(i)], pzsend.at[i], pzrecv.at[zpeer(i)],
               device(x, b, zpeer(i), half)).wait_recv()
    vsum[...] = jnp.sum(vz[...], axis=0)
    vy[half, b] = vsum[...]
    py = [
        remote(vsum, vy.at[half, b], pysend.at[0, i], pyrecv.at[half, b],
               device(x, bpeer(i), z, half))
        for i in range(1, nb)
    ]
    py += [
        remote(vsum, vy.at[half, b], pysend.at[1, i], pyrecv.at[half, b],
               device(x, bpeer(i), z, 1 - half))
        for i in range(nb)
    ]
    for copy in py:
        copy.start()

    for s in range(2 * nz):
        dg[:, s * feats : s * feats + head] = dgp[s, :, 0:head]
        dg[:, s * feats + head : (s + 1) * feats] = dgp[s, :, LANES : 2 * LANES]
    stores.append(pltpu.make_async_copy(dg, dg_hbm.at[0], store_sem.at[2]))
    stores[-1].start()

    for i in range(1, nb):
        remote(vsum, vy.at[half, bpeer(i)], pysend.at[0, i], pyrecv.at[half, bpeer(i)],
               device(x, bpeer(i), z, half)).wait_recv()
    for i in range(nb):
        remote(vsum, vy.at[1 - half, bpeer(i)], pysend.at[1, i],
               pyrecv.at[1 - half, bpeer(i)], device(x, bpeer(i), z, 1 - half)).wait_recv()
    mine = iota((nb, LANES), 0) == b
    for i in range(nb):
        both = vy[0, i] + vy[1, i]
        usum[i : i + 1, :] = jnp.sum(jnp.where(mine, both, 0.0), axis=0, keepdims=True)
    vx[x] = usum[...]
    px = [
        remote(usum, vx.at[x], pxsend.at[i], pxrecv.at[x], device(xpeer(i), b, z, half))
        for i in range(1, nx)
    ]
    for copy in px:
        copy.start()
    for i in range(1, nx):
        remote(usum, vx.at[xpeer(i)], pxsend.at[i], pxrecv.at[xpeer(i)],
               device(xpeer(i), b, z, half)).wait_recv()
    table = vx[...].reshape(nx * nb, LANES)
    token_probe = []
    for k in range(2):
        picked = (iota((tokens, nx * nb), 1) == ei[:, k : k + 1]).astype(F32)
        found = dot(picked, table, precision=lax.Precision.HIGHEST)
        lane = x * cap + si[:, k : k + 1]
        token_probe.append(
            jnp.sum(jnp.where(iota((tokens, LANES), 1) == lane, found, 0.0), axis=1, keepdims=True)
        )
    slope = (token_probe[0] - token_probe[1]) * share * (1.0 - share)
    rg[:, 0:1] = slope
    rg[:, 1:2] = -slope

    for c in range(2):
        for copy in xcopies[c]:
            copy.wait_send()
        for h in range(2):
            for copy in ycopies[h][c]:
                copy.wait_send()
    for copy in zcopies + pz + py + px:
        copy.wait_send()
    for copy in stores:
        copy.wait()


def shards(dims, out_grad, router_logits, expert_ids, slot_ids, down_weight, gate_pre, up_pre):
    nx, ny, nc, nz, cap = dims
    nb = ny * nc
    rows = nx * nb * cap
    tokens, feats = out_grad.shape
    hidden, width = down_weight.shape[1:]
    vmem = pl.BlockSpec(memory_space=pltpu.VMEM)
    hbm = pl.BlockSpec(memory_space=pl.ANY)
    dma = pltpu.SemaphoreType.DMA
    return pl.pallas_call(
        functools.partial(kernel, dims),
        out_shape=(
            jax.ShapeDtypeStruct(down_weight.shape, BF16),
            jax.ShapeDtypeStruct(gate_pre.shape, BF16),
            jax.ShapeDtypeStruct(up_pre.shape, BF16),
            jax.ShapeDtypeStruct(router_logits.shape, F32),
        ),
        in_specs=[vmem] * 4 + [hbm] * 3,
        out_specs=(hbm, hbm, hbm, vmem),
        scratch_shapes=[
            pltpu.VMEM((hidden, width), BF16),
            pltpu.VMEM((rows, hidden), BF16),
            pltpu.VMEM((rows, hidden), BF16),
            pltpu.VMEM((hidden, width), BF16),
            pltpu.VMEM((rows, hidden), BF16),
            pltpu.VMEM((rows, hidden), BF16),
            pltpu.VMEM((rows, rows), BF16),
            pltpu.VMEM((2, tokens, 2 * LANES), BF16),
            pltpu.VMEM((2, nx, nb * cap, LANES), BF16),
            pltpu.VMEM((2, nx, nb * cap, LANES), BF16),
            pltpu.VMEM((2, nb, nx * cap, LANES), BF16),
            pltpu.VMEM((2, 2, nb, nx * cap, LANES), BF16),
            pltpu.VMEM((nz, 4, rows, LANES), BF16),
            pltpu.VMEM((2 * nz, hidden, 2 * LANES), BF16),
            pltpu.VMEM((2 * nz, hidden, 2 * LANES), BF16),
            pltpu.VMEM((rows, hidden), F32),
            pltpu.VMEM((rows, hidden), F32),
            pltpu.VMEM((rows, hidden), F32),
            pltpu.VMEM((rows, hidden), F32),
            pltpu.VMEM((hidden, rows), BF16),
            pltpu.VMEM((nz, nb, LANES), F32),
            pltpu.VMEM((2, nb, nb, LANES), F32),
            pltpu.VMEM((nx, nb, LANES), F32),
            pltpu.VMEM((nb, LANES), F32),
            pltpu.VMEM((nb, LANES), F32),
            dma((3,)),
            dma((3,)),
            dma((2, nx)),
            dma((2, nx)),
            dma((2, 2, nb)),
            dma((2, 2, nb)),
            dma((2, 4, nz)),
            dma((4, nz)),
            dma((nz,)),
            dma((nz,)),
            dma((2, nb)),
            dma((2, nb)),
            dma((nx,)),
            dma((nx,)),
        ],
        compiler_params=pltpu.CompilerParams(
            collective_id=0, has_side_effects=True, vmem_limit_bytes=48 * 1024 * 1024
        ),
    )(out_grad, router_logits, expert_ids, slot_ids, down_weight, gate_pre, up_pre)


def solution(mesh, dims=(8, 4, 2, 8, 12)):
    placed = (
        P("expert", "tensor"),
        P("expert", None),
        P("expert", None),
        P("expert", None),
        P("expert", "tensor", None),
        P("expert", None, "tensor"),
        P("expert", None, "tensor"),
    )
    return jax.shard_map(
        functools.partial(shards, dims),
        mesh=mesh,
        in_specs=placed,
        out_specs=(
            P("expert", "tensor", None),
            P("expert", None, "tensor"),
            P("expert", None, "tensor"),
            P("expert", None),
        ),
        check_vma=False,
    )
```

time: 352 us -> 142 us (0.40)
  waiting for transfers between devices: 161 us -> 0 us
  blocking collectives: 154 us -> 0 us
  Pallas kernels: 0 us -> 128 us
  between operations: 14.2 us -> 0.72 us
  matrix products: 10.7 us -> 0 us
  local copies, waits for them, and re-layouts: 2.94 us -> 13.2 us
  starting transfers between devices: 4.73 us -> 0 us
  other arithmetic: 3.78 us -> 0 us
    all_gather x1 -> x0, waiting for transfers between devices: 152 us -> none  [shards(): full_rows = lax.all_gather(grad_rows, 'tensor', axis=1, tiled=True)]
    pallas_call x0 -> x1, Pallas kernels: none -> 128 us  [shards(): pl.pallas_call(functools.partial(kernel, dims), out_shape=(jax.ShapeDtype...]
    psum x1 -> x0, blocking collectives: 77.9 us -> none  [shards(): total_probe = lax.psum(row_probe, 'tensor')]
    all_to_all x2 -> x0, blocking collectives: 76.5 us -> none  [the longest x1 41.2 us: shards(): lax.all_to_all(total_probe.reshape(expert_count, capacity), 'expert', spl...]
    dot_general x4 -> x0, matrix products: 10.7 us -> none  [the longest x1 5.48 us: shards(): lax.dot_general(scaled, full_rows, (((0,), (0,)), ((), ())), preferred_el...]
    all_to_all x1 -> x0, waiting for transfers between devices: 9.08 us -> none  [shards(): lax.all_to_all(outgoing_weight.reshape(expert_count, capacity), 'expert',...]
    unnamed x8 -> x17, local copies, waits for them, and re-layouts: 0.03 us -> 7.94 us
    pallas_call x0 -> x3, local copies, waits for them, and re-layouts: none -> 5.22 us  [shards(): pl.pallas_call(functools.partial(kernel, dims), out_shape=(jax.ShapeDtype...]
  transfers between devices with their start and end apart: 2 -> 0, of which waited for: 2 -> 0; matrix products, arithmetic and copies ran while one was open for 0% -> 0% of each run, Pallas kernels for 0% -> 0%
where the time goes in v1:
time: 142 us
  Pallas kernels  128 us (90%)
  local copies, waits for them, and re-layouts  13.2 us (9%)
    pallas_call x1, Pallas kernels, shards(): pl.pallas_call(functools.partial(kernel, dims), out_shape=(jax.ShapeDtype...  128 us
    unnamed x17, local copies, waits for them, and re-layouts  7.94 us
    pallas_call x3, local copies, waits for them, and re-layouts, shards(): pl.pallas_call(functools.partial(kernel, dims), out_shape=(jax.ShapeDtype...  5.22 us

profile of v1, /device:TPU:1, one launch (start us, length us, event | category | flops | bytes accessed | tf_op | source)
XLA Modules:
  0.0 141.5 jit_solution(16112944338130454217)
XLA Ops:
  0.6 0.0 copy-start.4
  0.6 0.0 copy-start
  0.7 1.1 copy.11.og
  1.8 0.8 copy.12.rl
  2.6 0.8 copy.13.ei
  3.4 0.8 copy.14.si
  4.2 1.1 copy.15.gp_hbm
  5.3 0.0 copy-done.4
  5.3 0.2 copy.16.up_hbm
  5.5 0.0 copy-done
  5.5 127.6 %shard_map.102 = (bf16[1,152,3584]{2,1,0:T(8,128)(2,1)S(1)}, bf16[1,768,152]{2,1,0:T(8,128)(2,1)S(1)}, bf16[1,768,152]{2,1,0:T(8,128)(2,1)S(1)}, f32[256,2]{1,0:T(8,128)S(1)}) custom-call(bf16[256,224]{1,0:T(8,128)(2,1)S(1)} %copy.11.og, f32[256,2]{1,0:T(8,128)S(1)} %copy.12.rl, s32[256,2]{1,0:T(8,128)S(1)} %copy.13.ei, s32[256,2]{1,0:T(8,128)S(1)} %copy.14.si, ...), custom_call_target="tpu_custom_call" | custom-call | tf_op jit(solution)/shard_map/pallas_call | solution.py:317
  133.2 0.0 copy-start.1
  133.2 0.7 copy-done.1
  133.9 0.0 copy-start.2
  133.9 0.7 copy-done.2
  134.7 0.0 copy-start.3
  134.7 0.7 copy-done.3
  135.3 1.6 %copy.19 = f32[256,2]{0,1:T(2,128)} copy(f32[256,2]{1,0:T(8,128)} %copy-done.3) | data formatting | bytes 4096 | tf_op jit(solution)/shard_map/pallas_call | solution.py:317
  136.9 1.8 %copy.17 = bf16[1,768,152]{1,2,0:T(8,128)(2,1)} copy(bf16[1,768,152]{2,1,0:T(8,128)(2,1)} %copy-done.2) | data formatting | bytes 466944 | tf_op jit(solution)/shard_map/pallas_call | solution.py:317
  138.7 1.8 %copy.18 = bf16[1,768,152]{1,2,0:T(8,128)(2,1)} copy(bf16[1,768,152]{2,1,0:T(8,128)(2,1)} %copy-done.1) | data formatting | bytes 466944 | tf_op jit(solution)/shard_map/pallas_call | solution.py:317
  140.5 1.0 copy.21
Async XLA Ops:
  0.6 4.7 %copy-start.4 = (bf16[1,768,152]{1,2,0:T(8,128)(2,1)S(1)}, bf16[1,768,152]{1,2,0:T(8,128)(2,1)}, u32[]{:S(2)}) copy-start(bf16[1,768,152]{1,2,0:T(8,128)(2,1)} %param.13) | copy-start | bytes 700420
  0.6 4.9 %copy-start = (bf16[1,152,3584]{2,1,0:T(8,128)(2,1)S(1)}, bf16[1,152,3584]{2,1,0:T(8,128)(2,1)}, u32[]{:S(2)}) copy-start(bf16[1,152,3584]{2,1,0:T(8,128)(2,1)} %w_hbm.1) | copy-start | bytes 3268612
  133.2 0.7 copy-start.1
  133.9 0.7 copy-start.2
  134.7 0.7 copy-start.3

commit v2 on v1

v2 whole, which is shorter than its diff:
```python
import contextlib
import functools

import jax
import jax.numpy as jnp
from jax import lax
from jax.experimental import pallas as pl
from jax.experimental.pallas import tpu as pltpu
from jax.sharding import PartitionSpec as P

MESH = pl.DeviceIdType.MESH
BF16 = jnp.bfloat16
F32 = jnp.float32
LANES = 128
VMEM_BYTES = 62 * 1024 * 1024


def dot(a, b, contract=((1,), (0,)), precision=None):
    return lax.dot_general(
        a, b, (contract, ((), ())), preferred_element_type=F32, precision=precision
    )


def iota(shape, dim):
    return lax.broadcasted_iota(jnp.int32, shape, dim)


def scope(name):
    return contextlib.nullcontext()


def kernel(
    dims, og_hbm, rl_hbm, ei_hbm, si_hbm, w_hbm, gp_hbm, up_hbm,
    dg_hbm, gg_hbm, ug_hbm, rg_hbm,
    og, rl, ei, si, w, gp, up, dg, gg, ug, rg,
    perm, spread, ext, xs, xr, ys, yr, g0, g1, unpacked, sw, wp, dgp, hid, act, f1, f2, scaled_t,
    vz, vy, vx, vsum, usum, load_sem, store_sem,
    xsend, xrecv, ysend, yrecv, zsend, zrecv, pzsend, pzrecv, pysend, pyrecv, pxsend, pxrecv,
):
    nx, ny, nc, nz, cap = dims
    nb = ny * nc
    group = nb * cap
    rows = nx * group
    feats = og.shape[0]
    head = feats - LANES
    hidden = w.shape[0]
    e, t = lax.axis_index("expert"), lax.axis_index("tensor")
    x, b = e // nb, e % nb
    z, half = t // 2, t % 2

    def xpeer(i):
        return lax.rem(x + i, nx)

    def bpeer(i):
        return lax.rem(b + i, nb)

    def zpeer(i):
        return lax.rem(z + i + nz, nz)

    def device(x_, b_, z_, half_):
        return {"expert": x_ * nb + b_, "tensor": z_ * 2 + half_}

    def remote(src, dst, send, recv, where):
        return pltpu.make_async_remote_copy(
            src_ref=src, dst_ref=dst, send_sem=send, recv_sem=recv,
            device_id=where, device_id_type=MESH,
        )

    loads = [
        pltpu.make_async_copy(src, dst, load_sem.at[n])
        for n, (src, dst) in enumerate(
            [
                (ei_hbm, ei), (si_hbm, si), (rl_hbm, rl), (og_hbm, og),
                (gp_hbm.at[0], gp), (up_hbm.at[0], up), (w_hbm.at[0], w),
            ]
        )
    ]
    for copy in loads:
        copy.start()

    barrier = pltpu.get_barrier_semaphore()
    peers = [device(xpeer(i), b, z, half) for i in range(1, nx)]
    peers += [device(x, bpeer(i), z, half) for i in range(1, nb)]
    peers += [device(x, bpeer(i), z, 1 - half) for i in range(nb)]
    peers += [device(x, b, zpeer(i), half) for i in range(1, nz)]
    for peer in peers:
        pl.semaphore_signal(barrier, inc=1, device_id=peer, device_id_type=MESH)

    for copy in loads[:4]:
        copy.wait()

    tokens = og.shape[1]
    share = jax.nn.sigmoid(rl[0:1, :] - rl[1:2, :])
    combine = [share.astype(BF16).astype(F32), (1.0 - share).astype(BF16).astype(F32)]
    chosen = []
    for k in range(2):
        ext[k, 0:head] = og[0:head]
        ext[k, LANES : 2 * LANES] = og[head:feats]
        ext[k, head:LANES] = jnp.where(
            iota((LANES - head, tokens), 0) == 0, combine[k], 0.0
        ).astype(BF16)
        slot = ei[k : k + 1] * cap + si[k : k + 1]
        chosen.append((iota((rows, tokens), 0) == slot).astype(F32).astype(BF16))

    xcopies = []
    for c in range(2):
        cols = slice(c * LANES, (c + 1) * LANES)
        outgoing = dot(chosen[0], ext[0, cols], ((1,), (1,)))
        outgoing += dot(chosen[1], ext[1, cols], ((1,), (1,)))
        xs[c] = outgoing.astype(BF16).reshape(nx, group, LANES)
        if c == 0:
            pl.semaphore_wait(barrier, len(peers))
        xcopies.append([
            remote(xs.at[c, xpeer(i)], xr.at[c, x], xsend.at[c, i], xrecv.at[c, x],
                   device(xpeer(i), b, z, half))
            for i in range(1, nx)
        ])
        for copy in xcopies[c]:
            copy.start()

    i_row = iota((rows, 1), 0)
    major = i_row // (nx * cap)
    rest = i_row - major * (nx * cap)
    minor = rest // cap
    source = minor * group + major * cap + (rest - minor * cap)
    perm[...] = (iota((rows, rows), 1) == source).astype(F32).astype(BF16)

    ycopies = [[None, None], [None, None]]
    for c in range(2):
        xr[c, x] = xs[c, x]
        with scope("x wait"):
            for i in range(1, nx):
                remote(xs.at[c, x], xr.at[c, xpeer(i)], xsend.at[c, i], xrecv.at[c, xpeer(i)],
                       device(xpeer(i), b, z, half)).wait_recv()
        turned = dot(perm[...], xr[c].reshape(rows, LANES)).astype(BF16)
        ys[c] = turned.reshape(nb, nx * cap, LANES)
        yr[0, c, b] = ys[c, b]
        ycopies[0][c] = [
            remote(ys.at[c, bpeer(i)], yr.at[0, c, b], ysend.at[0, c, i], yrecv.at[0, c, b],
                   device(x, bpeer(i), z, half))
            for i in range(1, nb)
        ]
        for copy in ycopies[0][c]:
            copy.start()
    for c in range(2):
        ycopies[1][c] = [
            remote(ys.at[c, bpeer(i)], yr.at[1, c, b], ysend.at[1, c, i], yrecv.at[1, c, b],
                   device(x, bpeer(i), z, 1 - half))
            for i in range(nb)
        ]
        for copy in ycopies[1][c]:
            copy.start()

    longer, shorter = nz // 2, nz - 1 - nz // 2
    hops = [(longer, shorter), (shorter, longer), (shorter, longer), (longer, shorter)]
    zcopies = []

    packs = LANES // (LANES - head)
    part = rows // packs

    def zref(q, src):
        return (g1 if q % 2 else g0).at[src, q // 2]

    def zsend_start(q, src, way):
        to = zpeer(1) if way == 0 else zpeer(-1)
        copy = remote(zref(q, src), zref(q, src), zsend.at[way, q, src], zrecv.at[q, src],
                      device(x, b, to, half))
        copy.start()
        zcopies.append(copy)

    def zwait(q, src):
        remote(zref(q, src), zref(q, src), zsend.at[0, q, src], zrecv.at[q, src],
               device(x, b, zpeer(1), half)).wait_recv()

    hid[...] = jnp.zeros_like(hid)
    unpacked[...] = jnp.zeros_like(unpacked)

    def work(q, src):
        h, c = q // 2, q % 2
        shard = src * 2 + (half if h == 0 else 1 - half)
        if c == 0:
            for n in range(packs):
                unpacked[n * part : (n + 1) * part, 0:head] = g0[
                    src, h, :, n * head : (n + 1) * head
                ]
        block = unpacked[...] if c == 0 else g1[src, h]
        cols = slice(c * LANES, (c + 1) * LANES)
        hid[...] += dot(wp[shard, :, cols], block, ((1,), (1,)))
        dgp[shard, :, cols] = dot(scaled_t[...], block).astype(BF16)

    for d in range(4 + nz // 2):
        ready = []
        if d < 4:
            h, c = d // 2, d % 2
            with scope("y wait"):
                for i in range(1 if h == 0 else 0, nb):
                    remote(ys.at[c, b], yr.at[h, c, bpeer(i)], ysend.at[h, c, i],
                           yrecv.at[h, c, bpeer(i)], device(x, bpeer(i), z, half)).wait_recv()
            canon = dot(perm[...], yr[h, c].reshape(rows, LANES),
                        ((0,), (0,)) if nx != nb else ((1,), (0,)))
            canon = canon.astype(BF16)
            if c == 0:
                for n in range(packs):
                    g0[z, h, :, n * head : (n + 1) * head] = canon[
                        n * part : (n + 1) * part, 0:head
                    ]
            else:
                g1[z, h] = canon
            zsend_start(d, z, 0)
            zsend_start(d, z, 1)
            ready.append((d, z))
        for q in range(4):
            s = d - q
            if s < 1:
                continue
            for way in range(2):
                if s <= hops[q][way]:
                    src = zpeer(-s) if way == 0 else zpeer(s)
                    with scope("z wait"):
                        zwait(q, src)
                    if s < hops[q][way]:
                        zsend_start(q, src, way)
                    ready.append((q, src))
        if d == 0:
            pick = (iota((8, LANES), 1) == head).astype(F32).astype(BF16)
            sw[...] = dot(pick, canon, ((1,), (1,)))[0:1]
            for copy in loads[4:]:
                copy.wait()
            for s in range(2 * nz):
                wp[s, :, 0:head] = w[:, s * feats : s * feats + head]
                wp[s, :, head:LANES] = jnp.zeros((hidden, LANES - head), BF16)
                wp[s, :, LANES : 2 * LANES] = w[:, s * feats + head : (s + 1) * feats]
            held = ready
            continue
        if d == 1:
            slot_weight = sw[...]
            gate = gp[...].astype(F32)
            upf = up[...].astype(F32)
            sigma = jax.nn.sigmoid(gate)
            silu = gate * sigma
            act[...] = silu * upf
            scaled_t[...] = (slot_weight * act[...]).astype(BF16)
            f1[...] = slot_weight * (upf * (sigma * (1.0 + gate * (1.0 - sigma))))
            f2[...] = slot_weight * silu
            i_row = iota((rows, 1), 0)
            i_x = i_row // group
            i_rest = i_row - i_x * group
            i_b = i_rest // cap
            i_lane = i_x * cap + (i_rest - i_b * cap)
            spread[...] = (iota((rows, LANES), 1) == i_lane).astype(F32)
            ready = held + ready
        with scope("matmuls"):
            for q, src in ready:
                work(q, src)

    probe = jnp.sum(hid[...] * act[...], axis=0, keepdims=True)
    j_row = iota((1, rows), 1)
    j_rest = j_row - (j_row // group) * group
    parted = jnp.where(iota((nb, rows), 0) == j_rest // cap, probe, 0.0)
    vz[z] = dot(parted, spread[...], precision=lax.Precision.HIGHEST)
    pz = [
        remote(vz.at[z], vz.at[z], pzsend.at[i], pzrecv.at[z], device(x, b, zpeer(i), half))
        for i in range(1, nz)
    ]
    for copy in pz:
        copy.start()

    gg[...] = (hid[...] * f1[...]).astype(BF16)
    ug[...] = (hid[...] * f2[...]).astype(BF16)
    stores = [
        pltpu.make_async_copy(gg, gg_hbm.at[0], store_sem.at[0]),
        pltpu.make_async_copy(ug, ug_hbm.at[0], store_sem.at[1]),
    ]
    for copy in stores:
        copy.start()

    with scope("sum z wait"):
        for i in range(1, nz):
            remote(vz.at[z], vz.at[zpeer(i)], pzsend.at[i], pzrecv.at[zpeer(i)],
                   device(x, b, zpeer(i), half)).wait_recv()
    vsum[...] = jnp.sum(vz[...], axis=0)
    vy[half, b] = vsum[...]
    py = [
        remote(vsum, vy.at[half, b], pysend.at[0, i], pyrecv.at[half, b],
               device(x, bpeer(i), z, half))
        for i in range(1, nb)
    ]
    py += [
        remote(vsum, vy.at[half, b], pysend.at[1, i], pyrecv.at[half, b],
               device(x, bpeer(i), z, 1 - half))
        for i in range(nb)
    ]
    for copy in py:
        copy.start()

    for s in range(2 * nz):
        dg[:, s * feats : s * feats + head] = dgp[s, :, 0:head]
        dg[:, s * feats + head : (s + 1) * feats] = dgp[s, :, LANES : 2 * LANES]
    stores.append(pltpu.make_async_copy(dg, dg_hbm.at[0], store_sem.at[2]))
    stores[-1].start()

    with scope("sum y wait"):
        for i in range(1, nb):
            remote(vsum, vy.at[half, bpeer(i)], pysend.at[0, i], pyrecv.at[half, bpeer(i)],
                   device(x, bpeer(i), z, half)).wait_recv()
        for i in range(nb):
            remote(vsum, vy.at[1 - half, bpeer(i)], pysend.at[1, i],
                   pyrecv.at[1 - half, bpeer(i)], device(x, bpeer(i), z, 1 - half)).wait_recv()
    mine = iota((nb, LANES), 0) == b
    for i in range(nb):
        both = vy[0, i] + vy[1, i]
        usum[i : i + 1, :] = jnp.sum(jnp.where(mine, both, 0.0), axis=0, keepdims=True)
    vx[x] = usum[...]
    px = [
        remote(usum, vx.at[x], pxsend.at[i], pxrecv.at[x], device(xpeer(i), b, z, half))
        for i in range(1, nx)
    ]
    for copy in px:
        copy.start()
    with scope("sum x wait"):
        for i in range(1, nx):
            remote(usum, vx.at[xpeer(i)], pxsend.at[i], pxrecv.at[xpeer(i)],
                   device(xpeer(i), b, z, half)).wait_recv()
    table = vx[...].reshape(nx * nb, LANES)
    token_probe = []
    for k in range(2):
        picked = (iota((nx * nb, tokens), 0) == ei[k : k + 1]).astype(F32)
        found = dot(table, picked, ((0,), (0,)), precision=lax.Precision.HIGHEST)
        lane = x * cap + si[k : k + 1]
        token_probe.append(
            jnp.sum(jnp.where(iota((LANES, tokens), 0) == lane, found, 0.0), axis=0, keepdims=True)
        )
    slope = (token_probe[0] - token_probe[1]) * share * (1.0 - share)
    rg[0:1] = slope
    rg[1:2] = -slope
    stores.append(pltpu.make_async_copy(rg, rg_hbm, store_sem.at[3]))
    stores[-1].start()

    with scope("end"):
        for c in range(2):
            for copy in xcopies[c]:
                copy.wait_send()
            for h in range(2):
                for copy in ycopies[h][c]:
                    copy.wait_send()
        for copy in zcopies + pz + py + px:
            copy.wait_send()
        for copy in stores:
            copy.wait()


def write_kernel(dg_in, gg_in, ug_in, rg_in, dg, gg, ug, rg, dg_v, gg_v, ug_v, rg_v, sem_in, sem_out):
    pieces = []
    for source, held, target in (
        (dg_in, dg_v, dg), (gg_in, gg_v, gg), (ug_in, ug_v, ug), (rg_in, rg_v, rg)
    ):
        height = source.shape[-2]
        step = 80 if source is dg_in else height
        for at in range(0, height, step):
            piece = pl.ds(at, min(step, height - at))
            if len(source.shape) == 3:
                pieces.append((source.at[0, piece], held.at[0, piece], target.at[0, piece]))
            else:
                pieces.append((source, held, target))
    reads = [
        pltpu.make_async_copy(source, held, sem_in.at[n])
        for n, (source, held, _) in enumerate(pieces)
    ]
    writes = [
        pltpu.make_async_copy(held, target, sem_out.at[n])
        for n, (_, held, target) in enumerate(pieces)
    ]
    for read in reads:
        read.start()
    for read, write in zip(reads, writes):
        read.wait()
        write.start()
    for write in writes:
        write.wait()


def shards(dims, out_grad, router_logits, expert_ids, slot_ids, down_weight, gate_pre, up_pre):
    nx, ny, nc, nz, cap = dims
    nb = ny * nc
    rows = nx * nb * cap
    tokens, feats = out_grad.shape
    hidden, width = down_weight.shape[1:]
    head = feats - LANES
    packs = LANES // (LANES - head)
    hbm = pl.BlockSpec(memory_space=pl.ANY)
    dma = pltpu.SemaphoreType.DMA
    results = pl.pallas_call(
        functools.partial(kernel, dims),
        out_shape=(
            jax.ShapeDtypeStruct(down_weight.shape, BF16),
            jax.ShapeDtypeStruct((1, hidden, rows), BF16),
            jax.ShapeDtypeStruct((1, hidden, rows), BF16),
            jax.ShapeDtypeStruct((2, tokens), F32),
        ),
        in_specs=[hbm] * 7,
        out_specs=(hbm,) * 4,
        scratch_shapes=[
            pltpu.VMEM((feats, tokens), BF16),
            pltpu.VMEM((2, tokens), F32),
            pltpu.VMEM((2, tokens), jnp.int32),
            pltpu.VMEM((2, tokens), jnp.int32),
            pltpu.VMEM((hidden, width), BF16),
            pltpu.VMEM((hidden, rows), BF16),
            pltpu.VMEM((hidden, rows), BF16),
            pltpu.VMEM((hidden, width), BF16),
            pltpu.VMEM((hidden, rows), BF16),
            pltpu.VMEM((hidden, rows), BF16),
            pltpu.VMEM((2, tokens), F32),
            pltpu.VMEM((rows, rows), BF16),
            pltpu.VMEM((rows, LANES), F32),
            pltpu.VMEM((2, 2 * LANES, tokens), BF16),
            pltpu.VMEM((2, nx, nb * cap, LANES), BF16),
            pltpu.VMEM((2, nx, nb * cap, LANES), BF16),
            pltpu.VMEM((2, nb, nx * cap, LANES), BF16),
            pltpu.VMEM((2, 2, nb, nx * cap, LANES), BF16),
            pltpu.VMEM((nz, 2, rows // packs, packs * head), BF16),
            pltpu.VMEM((nz, 2, rows, LANES), BF16),
            pltpu.VMEM((rows, LANES), BF16),
            pltpu.VMEM((1, rows), F32),
            pltpu.VMEM((2 * nz, hidden, 2 * LANES), BF16),
            pltpu.VMEM((2 * nz, hidden, 2 * LANES), BF16),
            pltpu.VMEM((hidden, rows), F32),
            pltpu.VMEM((hidden, rows), F32),
            pltpu.VMEM((hidden, rows), F32),
            pltpu.VMEM((hidden, rows), F32),
            pltpu.VMEM((hidden, rows), BF16),
            pltpu.VMEM((nz, nb, LANES), F32),
            pltpu.VMEM((2, nb, nb, LANES), F32),
            pltpu.VMEM((nx, nb, LANES), F32),
            pltpu.VMEM((nb, LANES), F32),
            pltpu.VMEM((nb, LANES), F32),
            dma((7,)),
            dma((4,)),
            dma((2, nx)),
            dma((2, nx)),
            dma((2, 2, nb)),
            dma((2, 2, nb)),
            dma((2, 4, nz)),
            dma((4, nz)),
            dma((nz,)),
            dma((nz,)),
            dma((2, nb)),
            dma((2, nb)),
            dma((nx,)),
            dma((nx,)),
        ],
        compiler_params=pltpu.CompilerParams(
            collective_id=0, has_side_effects=True, vmem_limit_bytes=VMEM_BYTES
        ),
    )(
        out_grad.T, router_logits.T, expert_ids.T, slot_ids.T, down_weight,
        gate_pre.transpose(0, 2, 1), up_pre.transpose(0, 2, 1),
    )
    down_grad, gate_grad, up_grad, router_grad = pl.pallas_call(
        write_kernel,
        out_shape=tuple(jax.ShapeDtypeStruct(r.shape, r.dtype) for r in results),
        in_specs=[hbm] * 4,
        out_specs=(hbm,) * 4,
        scratch_shapes=[pltpu.VMEM(r.shape, r.dtype) for r in results] + [dma((5,)), dma((5,))],
        compiler_params=pltpu.CompilerParams(vmem_limit_bytes=VMEM_BYTES),
    )(*results)
    return (
        down_grad, gate_grad.transpose(0, 2, 1), up_grad.transpose(0, 2, 1), router_grad.T
    )


def solution(mesh, dims=(8, 4, 2, 8, 12)):
    placed = (
        P("expert", "tensor"),
        P("expert", None),
        P("expert", None),
        P("expert", None),
        P("expert", "tensor", None),
        P("expert", None, "tensor"),
        P("expert", None, "tensor"),
    )
    return jax.shard_map(
        functools.partial(shards, dims),
        mesh=mesh,
        in_specs=placed,
        out_specs=(
            P("expert", "tensor", None),
            P("expert", None, "tensor"),
            P("expert", None, "tensor"),
            P("expert", None),
        ),
        check_vma=False,
    )
```

time: 142 us -> 124 us (0.87)
  local copies, waits for them, and re-layouts: 13.2 us -> 0 us
  Pallas kernels: 128 us -> 124 us
    unnamed x17 -> x0, local copies, waits for them, and re-layouts: 7.94 us -> none
    pallas_call x1, Pallas kernels: 128 us -> 121 us  [shards(): pl.pallas_call(functools.partial(kernel, dims), out_shape=(jax.ShapeDtype...]
    pallas_call x3 -> x0, local copies, waits for them, and re-layouts: 5.22 us -> none  [shards(): pl.pallas_call(functools.partial(kernel, dims), out_shape=(jax.ShapeDtype...]
    pallas_call x0 -> x1, Pallas kernels: none -> 2.27 us  [shards(): pl.pallas_call(write_kernel, out_shape=tuple((jax.ShapeDtypeStruct(r.shap...]
where the time goes in v2:
time: 124 us
  Pallas kernels  124 us (100%)
    pallas_call x1, Pallas kernels, shards(): pl.pallas_call(functools.partial(kernel, dims), out_shape=(jax.ShapeDtype...  121 us

profile of v2, /device:TPU:1, one launch (start us, length us, event | category | flops | bytes accessed | tf_op | source)
XLA Modules:
  0.0 124.2 jit_solution(12248052926186664541)
XLA Ops:
  0.6 121.3 %shard_map.102 = (bf16[1,152,3584]{2,1,0:T(8,128)(2,1)}, bf16[1,152,768]{2,1,0:T(8,128)(2,1)}, bf16[1,152,768]{2,1,0:T(8,128)(2,1)}, f32[2,256]{1,0:T(2,128)}) custom-call(bf16[224,256]{1,0:T(8,128)(2,1)} %bitcast.11, f32[2,256]{1,0:T(2,128)} %bitcast.12, s32[2,256]{1,0:T(2,128)} %bitcast.13, s32[2,256]{1,0:T(2,128)} %bitcast.14, ...), custom_call_target="tpu_custom_call" | custom-call | tf_op jit(solution)/shard_map/pallas_call | solution.py:392
  121.9 2.3 %shard_map.103 = (bf16[1,152,3584]{2,1,0:T(8,128)(2,1)}, bf16[1,152,768]{2,1,0:T(8,128)(2,1)}, bf16[1,152,768]{2,1,0:T(8,128)(2,1)}, f32[2,256]{1,0:T(2,128)}) custom-call(bf16[1,152,3584]{2,1,0:T(8,128)(2,1)} %get-tuple-element.12.dg_in, bf16[1,152,768]{2,1,0:T(8,128)(2,1)} %get-tuple-element.13.gg_in, bf16[1,152,768]{2,1,0:T(8,128)(2,1)} %get-tuple-element.14.ug_in, ...), custom_call_target="tpu_custom_call" | custom-call | tf_op jit(solution)/shard_map/pallas_call | solution.py:459

commit v3 on v2

v3 whole, which is shorter than its diff:
```python
import functools

import jax
import jax.numpy as jnp
from jax import lax
from jax.experimental import pallas as pl
from jax.experimental.pallas import tpu as pltpu
from jax.sharding import PartitionSpec as P

MESH = pl.DeviceIdType.MESH
BF16 = jnp.bfloat16
F32 = jnp.float32
LANES = 128
VMEM_BYTES = 62 * 1024 * 1024


def dot(a, b, contract=((1,), (0,))):
    return lax.dot_general(a, b, (contract, ((), ())), preferred_element_type=F32)


def thirds(v):
    first = v.astype(BF16)
    rest = v - first.astype(F32)
    second = rest.astype(BF16)
    return [first, second, (rest - second.astype(F32)).astype(BF16)]


def iota(shape, dim):
    return lax.broadcasted_iota(jnp.int32, shape, dim)


def kernel(
    dims, og_hbm, rl_hbm, ei_hbm, si_hbm, w_hbm, gp_hbm, up_hbm,
    dg_hbm, gg_hbm, ug_hbm, rg_hbm,
    og, rl, ei, si, w, gp, up, dg, gg, ug, rg,
    perm, order, spread, ext, xs, xr, ys, yr, g0, g1, unpacked, sw, wp, dgp, hid, act, f1, f2,
    scaled, vz, vy, vx, vsum, usum, load_sem, store_sem,
    xsend, xrecv, ysend, yrecv, zsend, zrecv, pzsend, pzrecv, pysend, pyrecv, pxsend, pxrecv,
):
    nx, ny, nc, nz, cap = dims
    nb = ny * nc
    rows = nx * nb * cap
    part_cap = cap // 2
    part_rows = rows // 2
    part_group = nb * part_cap
    feats, tokens = og.shape
    head = feats - LANES
    packs = LANES // (LANES - head)
    packed_rows = part_rows // packs
    hidden = w.shape[0]
    e, t = lax.axis_index("expert"), lax.axis_index("tensor")
    x, b = e // nb, e % nb
    z, half = t // 2, t % 2

    def xpeer(i):
        return lax.rem(x + i, nx)

    def bpeer(i):
        return lax.rem(b + i, nb)

    def zpeer(i):
        return lax.rem(z + i + nz, nz)

    def device(x_, b_, z_, half_):
        return {"expert": x_ * nb + b_, "tensor": z_ * 2 + half_}

    def farthest(n):
        return sorted(range(1, n), key=lambda i: -min(i, n - i))

    def remote(src, dst, send, recv, where):
        return pltpu.make_async_remote_copy(
            src_ref=src, dst_ref=dst, send_sem=send, recv_sem=recv,
            device_id=where, device_id_type=MESH,
        )

    loads = [
        pltpu.make_async_copy(src, dst, load_sem.at[n])
        for n, (src, dst) in enumerate(
            [
                (ei_hbm, ei), (si_hbm, si), (rl_hbm, rl), (og_hbm, og),
                (gp_hbm.at[0], gp), (up_hbm.at[0], up), (w_hbm.at[0], w),
            ]
        )
    ]
    for copy in loads:
        copy.start()

    barrier = pltpu.get_barrier_semaphore()
    peers = [device(xpeer(i), b, z, half) for i in farthest(nx)]
    peers += [device(x, bpeer(i), z, half) for i in range(1, nb)]
    peers += [device(x, bpeer(i), z, 1 - half) for i in range(nb)]
    peers += [device(x, b, zpeer(i), half) for i in range(1, nz)]
    for peer in peers:
        pl.semaphore_signal(barrier, inc=1, device_id=peer, device_id_type=MESH)

    for copy in loads[:4]:
        copy.wait()

    share = jax.nn.sigmoid(rl[0:1, :] - rl[1:2, :])
    combine = [share.astype(BF16).astype(F32), (1.0 - share).astype(BF16).astype(F32)]
    chosen = [[], []]
    for k in range(2):
        ext[k, 0:head] = og[0:head]
        ext[k, LANES : 2 * LANES] = og[head:feats]
        ext[k, head:LANES] = jnp.where(
            iota((LANES - head, tokens), 0) == 0, combine[k], 0.0
        ).astype(BF16)
        for r in range(2):
            place = si[k : k + 1] - r * part_cap
            inside = (place >= 0) & (place < part_cap)
            row = jnp.where(inside, ei[k : k + 1] * part_cap + place, -1)
            chosen[r].append((iota((part_rows, tokens), 0) == row).astype(F32).astype(BF16))

    chunks = [(c, r) for c in range(2) for r in range(2)]
    xcopies = []
    for c, r in chunks:
        cols = slice(c * LANES, (c + 1) * LANES)
        outgoing = dot(chosen[r][0], ext[0, cols], ((1,), (1,)))
        outgoing += dot(chosen[r][1], ext[1, cols], ((1,), (1,)))
        xs[c, r] = outgoing.astype(BF16).reshape(nx, part_group, LANES)
        if (c, r) == (0, 0):
            pl.semaphore_wait(barrier, len(peers))
        for i in farthest(nx):
            copy = remote(xs.at[c, r, xpeer(i)], xr.at[c, r, x], xsend.at[c, r, i],
                          xrecv.at[c, r, x], device(xpeer(i), b, z, half))
            copy.start()
            xcopies.append(copy)

    i_row = iota((part_rows, 1), 0)
    major = i_row // (nx * part_cap)
    rest = i_row - major * (nx * part_cap)
    minor = rest // part_cap
    source = minor * part_group + major * part_cap + (rest - minor * part_cap)
    perm[...] = (iota((part_rows, part_rows), 1) == source).astype(F32).astype(BF16)

    n_lane = iota((1, rows), 1)
    n_part = n_lane // part_rows
    n_rest = n_lane - n_part * part_rows
    n_source = n_rest // part_cap
    n_slot = n_rest - n_source * part_cap
    origin = n_source * cap + n_part * part_cap + n_slot
    order[...] = (iota((rows, rows), 0) == origin).astype(F32).astype(BF16)

    i_row = iota((rows, 1), 0)
    i_part = i_row // part_rows
    i_rest = i_row - i_part * part_rows
    i_source = i_rest // part_cap
    i_lane = (i_source // nb) * cap + i_part * part_cap + (i_rest - i_source * part_cap)
    spread[...] = (iota((rows, LANES), 1) == i_lane).astype(F32).astype(BF16)

    for copy in loads[4:]:
        copy.wait()
    for s in range(2 * nz):
        wp[s, :, 0:head] = w[:, s * feats : s * feats + head]
        wp[s, :, head:LANES] = jnp.zeros((hidden, LANES - head), BF16)
        wp[s, :, LANES : 2 * LANES] = w[:, s * feats + head : (s + 1) * feats]
    gate = dot(gp[...], order[...])
    upf = dot(up[...], order[...])
    sigma = jax.nn.sigmoid(gate)
    silu = gate * sigma
    act[...] = silu * upf
    f1[...] = upf * (sigma * (1.0 + gate * (1.0 - sigma)))
    f2[...] = silu
    hid[...] = jnp.zeros_like(hid)
    unpacked[...] = jnp.zeros_like(unpacked)

    ycopies = []

    def ysend_start(c, r, h):
        for i in range(1 - h, nb):
            copy = remote(ys.at[c, r, bpeer(i)], yr.at[h, c, r, b], ysend.at[h, c, r, i],
                          yrecv.at[h, c, r, b],
                          device(x, bpeer(i), z, half if h == 0 else 1 - half))
            copy.start()
            ycopies.append(copy)

    for c, r in chunks:
        xr[c, r, x] = xs[c, r, x]
        for i in range(1, nx):
            remote(xs.at[c, r, x], xr.at[c, r, xpeer(i)], xsend.at[c, r, i],
                   xrecv.at[c, r, xpeer(i)], device(xpeer(i), b, z, half)).wait_recv()
        turned = dot(perm[...], xr[c, r].reshape(part_rows, LANES)).astype(BF16)
        ys[c, r] = turned.reshape(nb, nx * part_cap, LANES)
        yr[0, c, r, b] = ys[c, r, b]
        ysend_start(c, r, 0)

    longer, shorter = nz // 2, nz - 1 - nz // 2
    hops = [(longer, shorter), (shorter, longer), (shorter, longer), (longer, shorter)]
    zcopies = []

    def zref(q, src):
        h, c, r = q // 4, q // 2 % 2, q % 2
        return (g1 if c else g0).at[src, h, r]

    def zsend_start(q, src, way):
        to = zpeer(1) if way == 0 else zpeer(-1)
        copy = remote(zref(q, src), zref(q, src), zsend.at[way, q, src], zrecv.at[q, src],
                      device(x, b, to, half))
        copy.start()
        zcopies.append(copy)

    def zwait(q, src):
        remote(zref(q, src), zref(q, src), zsend.at[0, q, src], zrecv.at[q, src],
               device(x, b, zpeer(1), half)).wait_recv()

    def hidden_part(q, src):
        h, c = q // 4, q // 2 % 2
        shard = src * 2 + (half if h == 0 else 1 - half)
        if c == 0:
            for r in range(2):
                for n in range(packs):
                    at = r * part_rows + n * packed_rows
                    unpacked[at : at + packed_rows, 0:head] = g0[
                        src, h, r, :, n * head : (n + 1) * head
                    ]
            block = unpacked[...]
        else:
            block = g1[src, h].reshape(rows, LANES)
        hid[...] += dot(wp[shard, :, c * LANES : (c + 1) * LANES], block, ((1,), (1,)))
        return block, shard, slice(c * LANES, (c + 1) * LANES)

    def down_part(block, shard, cols):
        dgp[shard, :, cols] = dot(scaled[...], block).astype(BF16)

    def own(q):
        h, c, r = q // 4, q // 2 % 2, q % 2
        for i in range(1 - h, nb):
            remote(ys.at[c, r, b], yr.at[h, c, r, bpeer(i)], ysend.at[h, c, r, i],
                   yrecv.at[h, c, r, bpeer(i)], device(x, bpeer(i), z, half)).wait_recv()
        canon = dot(perm[...], yr[h, c, r].reshape(part_rows, LANES),
                    ((0,), (0,)) if nx != nb else ((1,), (0,))).astype(BF16)
        if c == 0:
            for n in range(packs):
                g0[z, h, r, :, n * head : (n + 1) * head] = canon[
                    n * packed_rows : (n + 1) * packed_rows, 0:head
                ]
        else:
            g1[z, h, r] = canon
        zsend_start(q, z, 0)
        zsend_start(q, z, 1)
        if q < 2:
            pick = (iota((8, LANES), 1) == head).astype(F32).astype(BF16)
            sw[:, q * part_rows : (q + 1) * part_rows] = dot(pick, canon, ((1,), (1,)))[0:1]

    steps = [(0, s) for s in range(nz // 2)] + [(1, 0), (0, nz // 2)]
    steps += [(1, s) for s in range(1, nz // 2 + 1)]
    later = []
    for n, (h, s) in enumerate(steps):
        done = []
        if s == 0:
            for q in range(4 * h, 4 * h + 4):
                own(q)
                if q % 2 == 1:
                    done.append((q, z))
            if h == 0:
                scaled[...] = (sw[...] * act[...]).astype(BF16)
                for c, r in chunks:
                    ysend_start(c, r, 1)
        else:
            for turn in range(2):
                for r in range(2):
                    for way in range(2):
                        c = turn if hops[2 * h][way] > hops[2 * h + 1][way] else 1 - turn
                        q = 4 * h + 2 * c + r
                        if s <= hops[2 * h + c][way]:
                            src = zpeer(-s) if way == 0 else zpeer(s)
                            zwait(q, src)
                            if s < hops[2 * h + c][way]:
                                zsend_start(q, src, way)
                            if r == 1:
                                done.append((q, src))
        for q, src in done:
            rest = hidden_part(q, src)
            if n < len(steps) - 1:
                down_part(*rest)
            else:
                later.append(rest)

    probe = jnp.sum(hid[...] * act[...], axis=0, keepdims=True)
    parted = jnp.where(iota((nb, rows), 0) == n_source - (n_source // nb) * nb, probe, 0.0)
    parts = dot(jnp.concatenate(thirds(parted), axis=0), spread[...])
    vz[z] = parts[0:nb] + parts[nb : 2 * nb] + parts[2 * nb : 3 * nb]
    pz = [
        remote(vz.at[z], vz.at[z], pzsend.at[i], pzrecv.at[z], device(x, b, zpeer(i), half))
        for i in farthest(nz)
    ]
    for copy in pz:
        copy.start()

    for rest in later:
        down_part(*rest)
    gg[...] = dot((hid[...] * (sw[...] * f1[...])).astype(BF16), order[...], ((1,), (1,))).astype(BF16)
    ug[...] = dot((hid[...] * (sw[...] * f2[...])).astype(BF16), order[...], ((1,), (1,))).astype(BF16)
    stores = [
        pltpu.make_async_copy(gg, gg_hbm.at[0], store_sem.at[0]),
        pltpu.make_async_copy(ug, ug_hbm.at[0], store_sem.at[1]),
    ]
    for copy in stores:
        copy.start()

    for i in range(1, nz):
        remote(vz.at[z], vz.at[zpeer(i)], pzsend.at[i], pzrecv.at[zpeer(i)],
               device(x, b, zpeer(i), half)).wait_recv()
    vsum[...] = jnp.sum(vz[...], axis=0)
    vy[half, b] = vsum[...]
    py = [
        remote(vsum, vy.at[half, b], pysend.at[1, i], pyrecv.at[half, b],
               device(x, bpeer(i), z, 1 - half))
        for i in range(nb)
    ]
    py += [
        remote(vsum, vy.at[half, b], pysend.at[0, i], pyrecv.at[half, b],
               device(x, bpeer(i), z, half))
        for i in range(1, nb)
    ]
    for copy in py:
        copy.start()

    for s in range(2 * nz):
        dg[:, s * feats : s * feats + head] = dgp[s, :, 0:head]
        dg[:, s * feats + head : (s + 1) * feats] = dgp[s, :, LANES : 2 * LANES]
    stores.append(pltpu.make_async_copy(dg, dg_hbm.at[0], store_sem.at[2]))
    stores[-1].start()

    for i in range(1, nb):
        remote(vsum, vy.at[half, bpeer(i)], pysend.at[0, i], pyrecv.at[half, bpeer(i)],
               device(x, bpeer(i), z, half)).wait_recv()
    for i in range(nb):
        remote(vsum, vy.at[1 - half, bpeer(i)], pysend.at[1, i],
               pyrecv.at[1 - half, bpeer(i)], device(x, bpeer(i), z, 1 - half)).wait_recv()
    mine = iota((nb, LANES), 0) == b
    for i in range(nb):
        both = vy[0, i] + vy[1, i]
        usum[i : i + 1, :] = jnp.sum(jnp.where(mine, both, 0.0), axis=0, keepdims=True)
    vx[x] = usum[...]
    px = [
        remote(usum, vx.at[x], pxsend.at[i], pxrecv.at[x], device(xpeer(i), b, z, half))
        for i in farthest(nx)
    ]
    for copy in px:
        copy.start()
    for i in range(1, nx):
        remote(usum, vx.at[xpeer(i)], pxsend.at[i], pxrecv.at[xpeer(i)],
               device(xpeer(i), b, z, half)).wait_recv()
    table = jnp.concatenate(thirds(vx[...].reshape(nx * nb, LANES)), axis=0)
    token_probe = []
    for k in range(2):
        picked = (iota((nx * nb, tokens), 0) == ei[k : k + 1]).astype(F32).astype(BF16)
        found = dot(table, jnp.concatenate([picked] * 3, axis=0), ((0,), (0,)))
        lane = x * cap + si[k : k + 1]
        token_probe.append(
            jnp.sum(jnp.where(iota((LANES, tokens), 0) == lane, found, 0.0), axis=0, keepdims=True)
        )
    slope = (token_probe[0] - token_probe[1]) * share * (1.0 - share)
    rg[0:1] = slope
    rg[1:2] = -slope
    stores.append(pltpu.make_async_copy(rg, rg_hbm, store_sem.at[3]))
    stores[-1].start()

    for copy in xcopies + ycopies + zcopies + pz + py + px:
        copy.wait_send()
    for copy in stores:
        copy.wait()


def write_kernel(dg_in, gg_in, ug_in, rg_in, dg, gg, ug, rg, dg_v, gg_v, ug_v, rg_v, sem_in, sem_out):
    pieces = []
    for source, held, target in (
        (dg_in, dg_v, dg), (gg_in, gg_v, gg), (ug_in, ug_v, ug), (rg_in, rg_v, rg)
    ):
        height = source.shape[-2]
        step = 80 if source is dg_in else height
        for at in range(0, height, step):
            piece = pl.ds(at, min(step, height - at))
            if len(source.shape) == 3:
                pieces.append((source.at[0, piece], held.at[0, piece], target.at[0, piece]))
            else:
                pieces.append((source, held, target))
    reads = [
        pltpu.make_async_copy(source, held, sem_in.at[n])
        for n, (source, held, _) in enumerate(pieces)
    ]
    writes = [
        pltpu.make_async_copy(held, target, sem_out.at[n])
        for n, (_, held, target) in enumerate(pieces)
    ]
    for read in reads:
        read.start()
    for read, write in zip(reads, writes):
        read.wait()
        write.start()
    for write in writes:
        write.wait()


def shards(dims, out_grad, router_logits, expert_ids, slot_ids, down_weight, gate_pre, up_pre):
    nx, ny, nc, nz, cap = dims
    nb = ny * nc
    rows = nx * nb * cap
    tokens, feats = out_grad.shape
    hidden, width = down_weight.shape[1:]
    head = feats - LANES
    packs = LANES // (LANES - head)
    hbm = pl.BlockSpec(memory_space=pl.ANY)
    dma = pltpu.SemaphoreType.DMA
    results = pl.pallas_call(
        functools.partial(kernel, dims),
        out_shape=(
            jax.ShapeDtypeStruct(down_weight.shape, BF16),
            jax.ShapeDtypeStruct((1, hidden, rows), BF16),
            jax.ShapeDtypeStruct((1, hidden, rows), BF16),
            jax.ShapeDtypeStruct((2, tokens), F32),
        ),
        in_specs=[hbm] * 7,
        out_specs=(hbm,) * 4,
        scratch_shapes=[
            pltpu.VMEM((feats, tokens), BF16),
            pltpu.VMEM((2, tokens), F32),
            pltpu.VMEM((2, tokens), jnp.int32),
            pltpu.VMEM((2, tokens), jnp.int32),
            pltpu.VMEM((hidden, width), BF16),
            pltpu.VMEM((hidden, rows), BF16),
            pltpu.VMEM((hidden, rows), BF16),
            pltpu.VMEM((hidden, width), BF16),
            pltpu.VMEM((hidden, rows), BF16),
            pltpu.VMEM((hidden, rows), BF16),
            pltpu.VMEM((2, tokens), F32),
            pltpu.VMEM((rows // 2, rows // 2), BF16),
            pltpu.VMEM((rows, rows), BF16),
            pltpu.VMEM((rows, LANES), BF16),
            pltpu.VMEM((2, 2 * LANES, tokens), BF16),
            pltpu.VMEM((2, 2, nx, nb * cap // 2, LANES), BF16),
            pltpu.VMEM((2, 2, nx, nb * cap // 2, LANES), BF16),
            pltpu.VMEM((2, 2, nb, nx * cap // 2, LANES), BF16),
            pltpu.VMEM((2, 2, 2, nb, nx * cap // 2, LANES), BF16),
            pltpu.VMEM((nz, 2, 2, rows // 2 // packs, packs * head), BF16),
            pltpu.VMEM((nz, 2, 2, rows // 2, LANES), BF16),
            pltpu.VMEM((rows, LANES), BF16),
            pltpu.VMEM((1, rows), F32),
            pltpu.VMEM((2 * nz, hidden, 2 * LANES), BF16),
            pltpu.VMEM((2 * nz, hidden, 2 * LANES), BF16),
            pltpu.VMEM((hidden, rows), F32),
            pltpu.VMEM((hidden, rows), F32),
            pltpu.VMEM((hidden, rows), F32),
            pltpu.VMEM((hidden, rows), F32),
            pltpu.VMEM((hidden, rows), BF16),
            pltpu.VMEM((nz, nb, LANES), F32),
            pltpu.VMEM((2, nb, nb, LANES), F32),
            pltpu.VMEM((nx, nb, LANES), F32),
            pltpu.VMEM((nb, LANES), F32),
            pltpu.VMEM((nb, LANES), F32),
            dma((7,)),
            dma((4,)),
            dma((2, 2, nx)),
            dma((2, 2, nx)),
            dma((2, 2, 2, nb)),
            dma((2, 2, 2, nb)),
            dma((2, 8, nz)),
            dma((8, nz)),
            dma((nz,)),
            dma((nz,)),
            dma((2, nb)),
            dma((2, nb)),
            dma((nx,)),
            dma((nx,)),
        ],
        compiler_params=pltpu.CompilerParams(
            collective_id=0, has_side_effects=True, vmem_limit_bytes=VMEM_BYTES
        ),
    )(
        out_grad.T, router_logits.T, expert_ids.T, slot_ids.T, down_weight,
        gate_pre.transpose(0, 2, 1), up_pre.transpose(0, 2, 1),
    )
    down_grad, gate_grad, up_grad, router_grad = pl.pallas_call(
        write_kernel,
        out_shape=tuple(jax.ShapeDtypeStruct(r.shape, r.dtype) for r in results),
        in_specs=[hbm] * 4,
        out_specs=(hbm,) * 4,
        scratch_shapes=[pltpu.VMEM(r.shape, r.dtype) for r in results] + [dma((5,)), dma((5,))],
        compiler_params=pltpu.CompilerParams(vmem_limit_bytes=VMEM_BYTES),
    )(*results)
    return (
        down_grad, gate_grad.transpose(0, 2, 1), up_grad.transpose(0, 2, 1), router_grad.T
    )


def solution(mesh, dims=(8, 4, 2, 8, 12)):
    placed = (
        P("expert", "tensor"),
        P("expert", None),
        P("expert", None),
        P("expert", None),
        P("expert", "tensor", None),
        P("expert", None, "tensor"),
        P("expert", None, "tensor"),
    )
    return jax.shard_map(
        functools.partial(shards, dims),
        mesh=mesh,
        in_specs=placed,
        out_specs=(
            P("expert", "tensor", None),
            P("expert", None, "tensor"),
            P("expert", None, "tensor"),
            P("expert", None),
        ),
        check_vma=False,
    )
```

time: 124 us -> 111 us (0.90)
  Pallas kernels: 124 us -> 110 us
    pallas_call x1, Pallas kernels: 121 us -> 108 us  [shards(): pl.pallas_call(functools.partial(kernel, dims), out_shape=(jax.ShapeDtype...]
where the time goes in v3:
time: 111 us
  Pallas kernels  110 us (99%)
    pallas_call x1, Pallas kernels, shards(): pl.pallas_call(functools.partial(kernel, dims), out_shape=(jax.ShapeDtype...  108 us
    pallas_call x1, Pallas kernels, shards(): pl.pallas_call(write_kernel, out_shape=tuple((jax.ShapeDtypeStruct(r.shap...  2.27 us

profile of v3, /device:TPU:1, one launch (start us, length us, event | category | flops | bytes accessed | tf_op | source)
XLA Modules:
  0.0 110.8 jit_solution(6321213613478941342)
XLA Ops:
  0.6 107.9 %shard_map.102 = (bf16[1,152,3584]{2,1,0:T(8,128)(2,1)}, bf16[1,152,768]{2,1,0:T(8,128)(2,1)}, bf16[1,152,768]{2,1,0:T(8,128)(2,1)}, f32[2,256]{1,0:T(2,128)}) custom-call(bf16[224,256]{1,0:T(8,128)(2,1)} %bitcast.11, f32[2,256]{1,0:T(2,128)} %bitcast.12, s32[2,256]{1,0:T(2,128)} %bitcast.13, s32[2,256]{1,0:T(2,128)} %bitcast.14, ...), custom_call_target="tpu_custom_call" | custom-call | tf_op jit(solution)/shard_map/pallas_call | solution.py:406
  108.5 2.3 %shard_map.103 = (bf16[1,152,3584]{2,1,0:T(8,128)(2,1)}, bf16[1,152,768]{2,1,0:T(8,128)(2,1)}, bf16[1,152,768]{2,1,0:T(8,128)(2,1)}, f32[2,256]{1,0:T(2,128)}) custom-call(bf16[1,152,3584]{2,1,0:T(8,128)(2,1)} %get-tuple-element.12.dg_in, bf16[1,152,768]{2,1,0:T(8,128)(2,1)} %get-tuple-element.13.gg_in, bf16[1,152,768]{2,1,0:T(8,128)(2,1)} %get-tuple-element.14.ug_in, ...), custom_call_target="tpu_custom_call" | custom-call | tf_op jit(solution)/shard_map/pallas_call | solution.py:474

commit v4 on v3

--- a/solution.py
+++ b/solution.py
@@ -35,7 +35,7 @@
     og, rl, ei, si, w, gp, up, dg, gg, ug, rg,
     perm, order, spread, ext, xs, xr, ys, yr, g0, g1, unpacked, sw, wp, dgp, hid, act, f1, f2,
     scaled, vz, vy, vx, vsum, usum, load_sem, store_sem,
-    xsend, xrecv, ysend, yrecv, zsend, zrecv, pzsend, pzrecv, pysend, pyrecv, pxsend, pxrecv,
+    xsend, xrecv, ysend, yrecv, zsend, zrecv, asend, arecv, pzsend, pzrecv, pysend, pyrecv, pxsend, pxrecv,
 ):
     nx, ny, nc, nz, cap = dims
     nb = ny * nc
@@ -185,7 +185,7 @@
         ysend_start(c, r, 0)
 
     longer, shorter = nz // 2, nz - 1 - nz // 2
-    hops = [(longer, shorter), (shorter, longer), (shorter, longer), (longer, shorter)]
+    hops = [(longer, shorter), (shorter, longer), (shorter, shorter), (shorter, shorter)]
     zcopies = []
 
     def zref(q, src):
@@ -203,23 +203,32 @@
         remote(zref(q, src), zref(q, src), zsend.at[0, q, src], zrecv.at[q, src],
                device(x, b, zpeer(1), half)).wait_recv()
 
-    def hidden_part(q, src):
+    def across(q, src):
+        return remote(zref(q, src), zref(q + 4, src), asend.at[q], arecv.at[q],
+                      device(x, b, z, 1 - half))
+
+    def block_of(q, src):
         h, c = q // 4, q // 2 % 2
-        shard = src * 2 + (half if h == 0 else 1 - half)
-        if c == 0:
-            for r in range(2):
-                for n in range(packs):
-                    at = r * part_rows + n * packed_rows
-                    unpacked[at : at + packed_rows, 0:head] = g0[
-                        src, h, r, :, n * head : (n + 1) * head
-                    ]
-            block = unpacked[...]
-        else:
-            block = g1[src, h].reshape(rows, LANES)
-        hid[...] += dot(wp[shard, :, c * LANES : (c + 1) * LANES], block, ((1,), (1,)))
-        return block, shard, slice(c * LANES, (c + 1) * LANES)
-
-    def down_part(block, shard, cols):
+        if c == 1:
+            return g1[src, h].reshape(rows, LANES)
+        for r in range(2):
+            for n in range(packs):
+                at = r * part_rows + n * packed_rows
+                unpacked[at : at + packed_rows, 0:head] = g0[
+                    src, h, r, :, n * head : (n + 1) * head
+                ]
+        return unpacked[...]
+
+    def place_of(q, src):
+        h, c = q // 4, q // 2 % 2
+        return src * 2 + (half if h == 0 else 1 - half), slice(c * LANES, (c + 1) * LANES)
+
+    def hidden_part(q, src, block):
+        shard, cols = place_of(q, src)
+        hid[...] += dot(wp[shard, :, cols], block, ((1,), (1,)))
+
+    def down_part(q, src, block):
+        shard, cols = place_of(q, src)
         dgp[shard, :, cols] = dot(scaled[...], block).astype(BF16)
 
     def own(q):
@@ -260,21 +269,30 @@
             for turn in range(2):
                 for r in range(2):
                     for way in range(2):
-                        c = turn if hops[2 * h][way] > hops[2 * h + 1][way] else 1 - turn
+                        c = turn if hops[2 * h][way] >= hops[2 * h + 1][way] else 1 - turn
                         q = 4 * h + 2 * c + r
                         if s <= hops[2 * h + c][way]:
                             src = zpeer(-s) if way == 0 else zpeer(s)
                             zwait(q, src)
                             if s < hops[2 * h + c][way]:
                                 zsend_start(q, src, way)
+                            if h == 0 and s == longer:
+                                copy = across(q, src)
+                                copy.start()
+                                zcopies.append(copy)
                             if r == 1:
                                 done.append((q, src))
+            if h == 1 and s == longer:
+                for q in range(4):
+                    across(q, zpeer(longer)).wait_recv()
+                done += [(5, zpeer(longer)), (7, zpeer(longer))]
         for q, src in done:
-            rest = hidden_part(q, src)
-            if n < len(steps) - 1:
-                down_part(*rest)
+            block = block_of(q, src)
+            hidden_part(q, src, block)
+            if n < len(steps) - 2:
+                down_part(q, src, block)
             else:
-                later.append(rest)
+                later.append((q, src))
 
     probe = jnp.sum(hid[...] * act[...], axis=0, keepdims=True)
     parted = jnp.where(iota((nb, rows), 0) == n_source - (n_source // nb) * nb, probe, 0.0)
@@ -287,8 +305,6 @@
     for copy in pz:
         copy.start()
 
-    for rest in later:
-        down_part(*rest)
     gg[...] = dot((hid[...] * (sw[...] * f1[...])).astype(BF16), order[...], ((1,), (1,))).astype(BF16)
     ug[...] = dot((hid[...] * (sw[...] * f2[...])).astype(BF16), order[...], ((1,), (1,))).astype(BF16)
     stores = [
@@ -316,6 +332,8 @@
     for copy in py:
         copy.start()
 
+    for q, src in later:
+        down_part(q, src, block_of(q, src))
     for s in range(2 * nz):
         dg[:, s * feats : s * feats + head] = dgp[s, :, 0:head]
         dg[:, s * feats + head : (s + 1) * feats] = dgp[s, :, LANES : 2 * LANES]
@@ -457,6 +475,8 @@
             dma((2, 2, 2, nb)),
             dma((2, 8, nz)),
             dma((8, nz)),
+            dma((4,)),
+            dma((4,)),
             dma((nz,)),
             dma((nz,)),
             dma((2, nb)),

time: 111 us -> 108 us (0.973)
  Pallas kernels: 110 us -> 107 us
    pallas_call x1, Pallas kernels: 108 us -> 104 us  [shards(): pl.pallas_call(functools.partial(kernel, dims), out_shape=(jax.ShapeDtype...]
where the time goes in v4:
time: 108 us; the launch traced here: 107 us
  Pallas kernels  107 us (99%)
    pallas_call x1, Pallas kernels, shards(): pl.pallas_call(functools.partial(kernel, dims), out_shape=(jax.ShapeDtype...  104 us
    pallas_call x1, Pallas kernels, shards(): pl.pallas_call(write_kernel, out_shape=tuple((jax.ShapeDtypeStruct(r.shap...  2.27 us

profile of v4, /device:TPU:1, one launch (start us, length us, event | category | flops | bytes accessed | tf_op | source)
XLA Modules:
  0.0 107.4 jit_solution(17744928408207470959)
XLA Ops:
  0.6 104.4 %shard_map.102 = (bf16[1,152,3584]{2,1,0:T(8,128)(2,1)}, bf16[1,152,768]{2,1,0:T(8,128)(2,1)}, bf16[1,152,768]{2,1,0:T(8,128)(2,1)}, f32[2,256]{1,0:T(2,128)}) custom-call(bf16[224,256]{1,0:T(8,128)(2,1)} %bitcast.11, f32[2,256]{1,0:T(2,128)} %bitcast.12, s32[2,256]{1,0:T(2,128)} %bitcast.13, s32[2,256]{1,0:T(2,128)} %bitcast.14, ...), custom_call_target="tpu_custom_call" | custom-call | tf_op jit(solution)/shard_map/pallas_call | solution.py:424
  105.0 2.3 %shard_map.103 = (bf16[1,152,3584]{2,1,0:T(8,128)(2,1)}, bf16[1,152,768]{2,1,0:T(8,128)(2,1)}, bf16[1,152,768]{2,1,0:T(8,128)(2,1)}, f32[2,256]{1,0:T(2,128)}) custom-call(bf16[1,152,3584]{2,1,0:T(8,128)(2,1)} %get-tuple-element.12.dg_in, bf16[1,152,768]{2,1,0:T(8,128)(2,1)} %get-tuple-element.13.gg_in, bf16[1,152,768]{2,1,0:T(8,128)(2,1)} %get-tuple-element.14.ug_in, ...), custom_call_target="tpu_custom_call" | custom-call | tf_op jit(solution)/shard_map/pallas_call | solution.py:494

commit v5 on v4

--- a/solution.py
+++ b/solution.py
@@ -387,7 +387,7 @@
         (dg_in, dg_v, dg), (gg_in, gg_v, gg), (ug_in, ug_v, ug), (rg_in, rg_v, rg)
     ):
         height = source.shape[-2]
-        step = 80 if source is dg_in else height
+        step = height
         for at in range(0, height, step):
             piece = pl.ds(at, min(step, height - at))
             if len(source.shape) == 3:

time: 108 us -> 108 us (level)
  no operation moved by 1% of the time
where the time goes in v5:
time: 108 us
  Pallas kernels  107 us (99%)
    pallas_call x1, Pallas kernels, shards(): pl.pallas_call(functools.partial(kernel, dims), out_shape=(jax.ShapeDtype...  104 us
    pallas_call x1, Pallas kernels, shards(): pl.pallas_call(write_kernel, out_shape=tuple((jax.ShapeDtypeStruct(r.shap...  2.45 us

profile of v5, /device:TPU:1, one launch (start us, length us, event | category | flops | bytes accessed | tf_op | source)
XLA Modules:
  0.0 107.6 jit_solution(18405946588246222854)
XLA Ops:
  0.6 104.4 %shard_map.102 = (bf16[1,152,3584]{2,1,0:T(8,128)(2,1)}, bf16[1,152,768]{2,1,0:T(8,128)(2,1)}, bf16[1,152,768]{2,1,0:T(8,128)(2,1)}, f32[2,256]{1,0:T(2,128)}) custom-call(bf16[224,256]{1,0:T(8,128)(2,1)} %bitcast.11, f32[2,256]{1,0:T(2,128)} %bitcast.12, s32[2,256]{1,0:T(2,128)} %bitcast.13, s32[2,256]{1,0:T(2,128)} %bitcast.14, ...), custom_call_target="tpu_custom_call" | custom-call | tf_op jit(solution)/shard_map/pallas_call | solution.py:424
  105.0 2.5 %shard_map.103 = (bf16[1,152,3584]{2,1,0:T(8,128)(2,1)}, bf16[1,152,768]{2,1,0:T(8,128)(2,1)}, bf16[1,152,768]{2,1,0:T(8,128)(2,1)}, f32[2,256]{1,0:T(2,128)}) custom-call(bf16[1,152,3584]{2,1,0:T(8,128)(2,1)} %get-tuple-element.12.dg_in, bf16[1,152,768]{2,1,0:T(8,128)(2,1)} %get-tuple-element.13.gg_in, bf16[1,152,768]{2,1,0:T(8,128)(2,1)} %get-tuple-element.14.ug_in, ...), custom_call_target="tpu_custom_call" | custom-call | tf_op jit(solution)/shard_map/pallas_call | solution.py:494
